TPU v7x, 32 devices: a whole 2x2x4 slice. The times are simulated.
32 devices in a mesh: row: 8 (over y, x, core), col: 4 (over z).
Axes of the slice: x: 2, y: 2, z: 4, core: 2. Of those that a mesh axis runs over, the one named last changes fastest.
Arguments:
- forcing_terms: float32 [8, 4, 2, 32, 128], P('row', 'col'), may hold values from -6 to 6
- diagonal_reciprocal: float32 [8, 4, 2, 128, 128], P('row', 'col'), may hold values from -0.5 to 0.5
- stiffness_submatrix: float32 [8, 4, 32, 128, 128], P('row', 'col'), may hold values from -0.1875 to 0.1875
- stiffness_source_index: int32 [8, 4, 32], P('row', 'col'), may hold values from 0 to 7
- stiffness_target_index: int32 [8, 4, 32], P('row', 'col'), may hold values from 0 to 15
- stiffness_nonzero_tally: int32 [8, 4], P('row', 'col'), may hold values from 1 to 32, as said below
- interpolant_submatrix: float32 [8, 4, 16, 128, 128], P('row', 'col'), may hold values from -0.125 to 0.125
- interpolant_cluster_index: int32 [8, 4, 16], P('row', 'col'), may hold values from 0 to 1
- interpolant_target_index: int32 [8, 4, 16], P('row', 'col'), may hold values from 0 to 15
- interpolant_nonzero_tally: int32 [8, 4], P('row', 'col'), may hold values from 1 to 16, as said below
- provisional_interpolant: float32 [8, 4, 2, 128], P('row', 'col'), may hold values from 0.2 to 1
- cluster_label: int32 [8, 4, 2, 128], P('row', 'col'), may hold values from 0 to 255
Outputs:
- relaxed_iterate: float32 [8, 4, 2, 32, 128], P('row', 'col')
- residual: float32 [8, 4, 2, 32, 128], P('row', 'col')
- coarse: float32 [8, 2, 32, 128], P('row')
Inputs may be any that keep to these rules, and one draw needn't show every extreme that they name: `stiffness_nonzero_tally`: tile slots at or past the count are unused; some pair has all 32 slots live in every draw. `interpolant_nonzero_tally`: tile slots at or past the count are unused; some pair has all 16 slots live in every draw.
All inputs are finite; a program needn't handle non-finite values.
Results may differ from a plain program's by a relative error of at most 0.0003.
Values sent between devices are 32-bit elements; how exact they have to be, the bound alone decides.
A program may use at most 64 MiB of HBM per device.

v0:
```python
import jax
import jax.numpy as jnp
from jax import lax
from jax.sharding import PartitionSpec as P

omega = 0.7
highest = lax.Precision.HIGHEST
tile_group = 8


def loop_tiles(blocks, stiffness_submatrices, rows, cols, low, high, nout):
    nrhs = blocks.shape[1]
    width = blocks.shape[2]

    def add_group(index, total):
        start = index * tile_group
        piece = lax.dynamic_slice_in_dim(stiffness_submatrices, start, tile_group, 0)
        row_ids = lax.dynamic_slice_in_dim(rows, start, tile_group, 0)
        col_ids = lax.dynamic_slice_in_dim(cols, start, tile_group, 0)
        slots = start + jnp.arange(tile_group)
        live = ((slots >= low) & (slots < high)).astype(jnp.float32)
        inputs = jnp.take(blocks, col_ids, axis=0)
        product = jnp.einsum("ska,sab->skb", inputs, piece, precision=highest)
        onehot = (row_ids[:, None] == jnp.arange(nout)[None, :]).astype(jnp.float32) * live[:, None]
        return total + jnp.einsum("so,skb->okb", onehot, product, precision=highest)

    starting_guess = low // tile_group
    last = (high + tile_group - 1) // tile_group
    empty = jnp.zeros((nout, nrhs, width), jnp.float32)
    return lax.fori_loop(starting_guess, last, add_group, empty)


def gather_columns(vec):
    whole = lax.all_gather(vec[None, None], "row", axis=0, tiled=True)
    return whole.reshape(-1, vec.shape[1], vec.shape[2])


def precondition(vec, inverse):
    return jnp.einsum("pka,pab->pkb", vec, inverse, precision=highest)


def stiffness_product(vec, stiffness_submatrices, rows, cols, count):
    blocks = gather_columns(vec)
    ncol = lax.axis_size("col")
    pblocks = vec.shape[0]
    nout = ncol * pblocks
    partial_value = loop_tiles(blocks, stiffness_submatrices, rows, cols, jnp.int32(0), count, nout)
    partial_value = partial_value.reshape(1, ncol, pblocks, vec.shape[1], vec.shape[2])
    pieces = lax.all_to_all(partial_value, "col", split_axis=1, concat_axis=0, tiled=True)
    return jnp.sum(pieces, axis=0)[0]


def body(
    forcing_terms,
    diagonal_reciprocal,
    stiffness_submatrix,
    stiffness_source_index,
    stiffness_target_index,
    stiffness_nonzero_tally,
    interpolant_submatrix,
    interpolant_cluster_index,
    interpolant_target_index,
    interpolant_nonzero_tally,
    provisional_interpolant,
    cluster_label,
):
    source = forcing_terms[0, 0]
    inverse = diagonal_reciprocal[0, 0]
    stiffness_submatrices = stiffness_submatrix[0, 0]
    rows = stiffness_source_index[0, 0]
    cols = stiffness_target_index[0, 0]
    count = stiffness_nonzero_tally[0, 0]
    starting_guess = omega * precondition(source, inverse)
    image_field = stiffness_product(starting_guess, stiffness_submatrices, rows, cols, count)
    relaxed_iterate = starting_guess + omega * precondition(source - image_field, inverse)
    image_field = stiffness_product(relaxed_iterate, stiffness_submatrices, rows, cols, count)
    residual = source - image_field
    pblocks, nrhs, width = residual.shape
    blocks = gather_columns(residual)
    part = loop_tiles(
        blocks,
        interpolant_submatrix[0, 0],
        interpolant_cluster_index[0, 0],
        interpolant_target_index[0, 0],
        jnp.int32(0),
        interpolant_nonzero_tally[0, 0],
        pblocks,
    )
    weighted = (
        (residual * provisional_interpolant[0, 0][:, None, :])
        .transpose(1, 0, 2)
        .reshape(nrhs, pblocks * width)
    )
    onehot = (
        cluster_label[0, 0].reshape(-1)[:, None] == jnp.arange(pblocks * width)[None, :]
    ).astype(jnp.float32)
    tentative = jnp.dot(weighted, onehot, precision=highest)
    part = part + tentative.reshape(nrhs, pblocks, width).transpose(1, 0, 2)
    coarse = lax.psum(part, "col")
    return (relaxed_iterate[None, None], residual[None, None], coarse[None])


def solution(mesh):
    placed = (
        P("row", "col", None, None, None),
        P("row", "col", None, None, None),
        P("row", "col", None, None, None),
        P("row", "col", None),
        P("row", "col", None),
        P("row", "col"),
        P("row", "col", None, None, None),
        P("row", "col", None),
        P("row", "col", None),
        P("row", "col"),
        P("row", "col", None, None),
        P("row", "col", None, None),
    )
    return jax.shard_map(
        body,
        mesh=mesh,
        in_specs=placed,
        out_specs=(
            P("row", "col", None, None, None),
            P("row", "col", None, None, None),
            P("row", None, None, None),
        ),
        check_vma=False,
    )
```

profile of v0, /device:TPU:0, one launch (start us, length us, event | category | flops | bytes accessed | tf_op | source)
XLA Modules:
  0.0 112.7 jit_solution(16195948218409422121)
XLA Ops:
  0.6 0.0 copy-start
  1.3 0.8 copy.69
  2.1 0.2 convolution_multiply_fusion.1
  2.4 10.8 %all-gather = f32[16,32,128]{2,1,0:T(8,128)S(1)} all-gather(f32[2,32,128]{2,1,0:T(8,128)S(1)} %convolution_multiply_fusion.1), channel_id=2, replica_groups=mesh['row'=8,'col'=4] {'row'}, dimensions={0}, use_global_device_ids=true | all-gather | bytes 294912 | tf_op jit(solution)/shard_map/all_gather | solution.py:34
  13.1 0.0 copy-start.2
  13.2 14.1 %while.30 = (s32[]{:T(128)}, f32[8,32,128]{2,0,1:T(8,128)S(1)}, s32[]{:T(128)}, s32[32]{0:T(128)}, s32[]{:T(128)}, /*index=5*/s32[32]{0:T(128)}, f32[16,32,128]{...) while((s32[]{:T(128)}, f32[8,32,128]{2,0,1:T(8,128)S(1)}, ...), condition=%wide.region_1.3_spmd, body=%wide.region_0.2_spmd.sunk | while | flops 53544156 | bytes 1446375 | solution.py:30
  13.2 1.4 %compare_and_fusion.6 = (pred[8]{0:T(512)(128)(4,1)S(1)}, s32[8]{0:T(128)S(1)}, f32[8]{0:T(128)S(1)}) fusion(s32[32]{0:T(128)} %get-tuple-element.396, s32[]{:T(128)S(6)} %select_n.65, s32[]{:T(128)} %get-tuple-element.395, s32[]{:T(128)S(6)} %mul.95), kind=kLoop, calls=%fused_computation.18.clone.1 | loop fusion | flops 88 | bytes 116 | tf_op jit(solution)/shard_map/while/body/jit(_take)/and | solution.py:22
  14.6 0.6 gather_fusion
  15.1 1.7 %fusion.74 = f32[8,32,128]{2,1,0:T(8,128)S(1)} fusion(f32[32,128,128]{2,1,0:T(8,128)} %get-tuple-element.398, s32[]{:T(128)S(6)} %select_n.65, f32[8,32,128]{2,1,0:T(8,128)S(1)} %gather_fusion, pred[8]{0:T(512)(128)(4,1)S(1)} %get-tuple-element.343), kind=kOutput, calls=%fused_computation.4.clone.1 | convolution fusion | flops 50364416 | bytes 786444 | tf_op jit(solution)/shard_map/while/body/ska,sab->skb/dot_general | solution.py:23
  16.8 0.7 dynamic_slice.46
  17.5 0.3 convolution_add_fusion.6
  17.9 1.4 %compare_and_fusion.6 = (pred[8]{0:T(512)(128)(4,1)S(1)}, s32[8]{0:T(128)S(1)}, f32[8]{0:T(128)S(1)}) fusion(s32[32]{0:T(128)} %get-tuple-element.396, s32[]{:T(128)S(6)} %select_n.65, s32[]{:T(128)} %get-tuple-element.395, s32[]{:T(128)S(6)} %mul.95), kind=kLoop, calls=%fused_computation.18.clone.1 | loop fusion | flops 88 | bytes 116 | tf_op jit(solution)/shard_map/while/body/jit(_take)/and | solution.py:22
  19.3 0.6 gather_fusion
  19.8 1.7 %fusion.74 = f32[8,32,128]{2,1,0:T(8,128)S(1)} fusion(f32[32,128,128]{2,1,0:T(8,128)} %get-tuple-element.398, s32[]{:T(128)S(6)} %select_n.65, f32[8,32,128]{2,1,0:T(8,128)S(1)} %gather_fusion, pred[8]{0:T(512)(128)(4,1)S(1)} %get-tuple-element.343), kind=kOutput, calls=%fused_computation.4.clone.1 | convolution fusion | flops 50364416 | bytes 786444 | tf_op jit(solution)/shard_map/while/body/ska,sab->skb/dot_general | solution.py:23
  21.5 0.7 dynamic_slice.46
  22.2 0.3 convolution_add_fusion.6
  22.6 1.4 %compare_and_fusion.6 = (pred[8]{0:T(512)(128)(4,1)S(1)}, s32[8]{0:T(128)S(1)}, f32[8]{0:T(128)S(1)}) fusion(s32[32]{0:T(128)} %get-tuple-element.396, s32[]{:T(128)S(6)} %select_n.65, s32[]{:T(128)} %get-tuple-element.395, s32[]{:T(128)S(6)} %mul.95), kind=kLoop, calls=%fused_computation.18.clone.1 | loop fusion | flops 88 | bytes 116 | tf_op jit(solution)/shard_map/while/body/jit(_take)/and | solution.py:22
  23.9 0.6 gather_fusion
  24.5 1.7 %fusion.74 = f32[8,32,128]{2,1,0:T(8,128)S(1)} fusion(f32[32,128,128]{2,1,0:T(8,128)} %get-tuple-element.398, s32[]{:T(128)S(6)} %select_n.65, f32[8,32,128]{2,1,0:T(8,128)S(1)} %gather_fusion, pred[8]{0:T(512)(128)(4,1)S(1)} %get-tuple-element.343), kind=kOutput, calls=%fused_computation.4.clone.1 | convolution fusion | flops 50364416 | bytes 786444 | tf_op jit(solution)/shard_map/while/body/ska,sab->skb/dot_general | solution.py:23
  26.2 0.7 dynamic_slice.46
  26.9 0.3 convolution_add_fusion.6
  27.2 0.7 copy.36
  27.9 3.9 %all-to-all-start = ((f32[1,4,2,32,128]{4,2,3,0,1:T(2,128)}), f32[1,4,2,32,128]{4,2,3,0,1:T(2,128)S(1)}, u32[]{:S(2)}, u32[]{:S(2)}) async-start(f32[1,4,2,32,128]{4,2,3,0,1:T(2,128)} %copy.36), calls=%async_computation | async-start | bytes 262144 | tf_op jit(solution)/shard_map/all_to_all | solution.py:49
  31.8 5.9 %all-to-all-done = f32[1,4,2,32,128]{4,2,3,0,1:T(2,128)S(1)} async-done(((f32[1,4,2,32,128]{4,2,3,0,1:T(2,128)}), f32[1,4,2,32,128]{4,2,3,0,1:T(2,128)S(1)}, u32[]{:S(2)}, u32[]{:S(2)}) %all-to-all-start) | async-done | bytes 131104 | tf_op jit(solution)/shard_map/all_to_all | solution.py:49
  37.7 0.1 reduce_sum.18
  37.8 0.2 fusion.45
  38.0 15.0 %all-gather.1 = f32[16,32,128]{2,1,0:T(8,128)S(1)} all-gather(f32[2,32,128]{2,1,0:T(8,128)S(1)} %fusion.45), channel_id=3, replica_groups=mesh['row'=8,'col'=4] {'row'}, dimensions={0}, use_global_device_ids=true | all-gather | bytes 294912 | tf_op jit(solution)/shard_map/all_gather | solution.py:34
  53.1 0.0 copy-start.1
  53.1 14.1 %while.31 = (s32[]{:T(128)}, f32[8,32,128]{2,0,1:T(8,128)S(1)}, s32[]{:T(128)}, s32[32]{0:T(128)}, s32[]{:T(128)}, /*index=5*/s32[32]{0:T(128)}, f32[16,32,128]{...) while((s32[]{:T(128)}, f32[8,32,128]{2,0,1:T(8,128)S(1)}, ...), condition=%wide.region_4.6_spmd, body=%wide.region_3.5_spmd.sunk | while | flops 53544156 | bytes 1446375 | solution.py:30
  53.1 1.5 %compare_and_fusion.7 = (pred[8]{0:T(512)(128)(4,1)S(1)}, s32[8]{0:T(128)S(1)}, f32[8]{0:T(128)S(1)}) fusion(s32[32]{0:T(128)} %get-tuple-element.432, s32[]{:T(128)S(6)} %select_n.67, s32[]{:T(128)} %get-tuple-element.431, s32[]{:T(128)S(6)} %mul.98), kind=kLoop, calls=%fused_computation.38.clone.1 | loop fusion | flops 88 | bytes 116 | tf_op jit(solution)/shard_map/while/body/jit(_take)/and | solution.py:22
  54.6 0.6 gather_fusion.1
  55.2 1.7 %fusion.79 = f32[8,32,128]{2,1,0:T(8,128)S(1)} fusion(f32[32,128,128]{2,1,0:T(8,128)} %get-tuple-element.434, s32[]{:T(128)S(6)} %select_n.67, f32[8,32,128]{2,1,0:T(8,128)S(1)} %gather_fusion.1, pred[8]{0:T(512)(128)(4,1)S(1)} %get-tuple-element.354), kind=kOutput, calls=%fused_computation.24.clone.1 | convolution fusion | flops 50364416 | bytes 786444 | tf_op jit(solution)/shard_map/while/body/ska,sab->skb/dot_general | solution.py:23
  56.8 0.7 dynamic_slice.48
  57.5 0.3 convolution_add_fusion.7
  57.9 1.4 %compare_and_fusion.7 = (pred[8]{0:T(512)(128)(4,1)S(1)}, s32[8]{0:T(128)S(1)}, f32[8]{0:T(128)S(1)}) fusion(s32[32]{0:T(128)} %get-tuple-element.432, s32[]{:T(128)S(6)} %select_n.67, s32[]{:T(128)} %get-tuple-element.431, s32[]{:T(128)S(6)} %mul.98), kind=kLoop, calls=%fused_computation.38.clone.1 | loop fusion | flops 88 | bytes 116 | tf_op jit(solution)/shard_map/while/body/jit(_take)/and | solution.py:22
  59.3 0.6 gather_fusion.1
  59.8 1.7 %fusion.79 = f32[8,32,128]{2,1,0:T(8,128)S(1)} fusion(f32[32,128,128]{2,1,0:T(8,128)} %get-tuple-element.434, s32[]{:T(128)S(6)} %select_n.67, f32[8,32,128]{2,1,0:T(8,128)S(1)} %gather_fusion.1, pred[8]{0:T(512)(128)(4,1)S(1)} %get-tuple-element.354), kind=kOutput, calls=%fused_computation.24.clone.1 | convolution fusion | flops 50364416 | bytes 786444 | tf_op jit(solution)/shard_map/while/body/ska,sab->skb/dot_general | solution.py:23
  61.5 0.7 dynamic_slice.48
  62.2 0.3 convolution_add_fusion.7
  62.6 1.4 %compare_and_fusion.7 = (pred[8]{0:T(512)(128)(4,1)S(1)}, s32[8]{0:T(128)S(1)}, f32[8]{0:T(128)S(1)}) fusion(s32[32]{0:T(128)} %get-tuple-element.432, s32[]{:T(128)S(6)} %select_n.67, s32[]{:T(128)} %get-tuple-element.431, s32[]{:T(128)S(6)} %mul.98), kind=kLoop, calls=%fused_computation.38.clone.1 | loop fusion | flops 88 | bytes 116 | tf_op jit(solution)/shard_map/while/body/jit(_take)/and | solution.py:22
  64.0 0.6 gather_fusion.1
  64.5 1.7 %fusion.79 = f32[8,32,128]{2,1,0:T(8,128)S(1)} fusion(f32[32,128,128]{2,1,0:T(8,128)} %get-tuple-element.434, s32[]{:T(128)S(6)} %select_n.67, f32[8,32,128]{2,1,0:T(8,128)S(1)} %gather_fusion.1, pred[8]{0:T(512)(128)(4,1)S(1)} %get-tuple-element.354), kind=kOutput, calls=%fused_computation.24.clone.1 | convolution fusion | flops 50364416 | bytes 786444 | tf_op jit(solution)/shard_map/while/body/ska,sab->skb/dot_general | solution.py:23
  66.2 0.7 dynamic_slice.48
  66.9 0.3 convolution_add_fusion.7
  67.2 0.7 copy.40
  67.9 3.3 %all-to-all-start.1 = ((f32[1,4,2,32,128]{4,2,3,0,1:T(2,128)}), f32[1,4,2,32,128]{4,2,3,0,1:T(2,128)S(1)}, u32[]{:S(2)}, u32[]{:S(2)}) async-start(f32[1,4,2,32,128]{4,2,3,0,1:T(2,128)} %copy.40), calls=%async_computation.1 | async-start | bytes 262144 | tf_op jit(solution)/shard_map/all_to_all | solution.py:49
  71.9 5.3 %all-to-all-done.1 = f32[1,4,2,32,128]{4,2,3,0,1:T(2,128)S(1)} async-done(((f32[1,4,2,32,128]{4,2,3,0,1:T(2,128)}), f32[1,4,2,32,128]{4,2,3,0,1:T(2,128)S(1)}, u32[]{:S(2)}, u32[]{:S(2)}) %all-to-all-start.1) | async-done | bytes 131104 | tf_op jit(solution)/shard_map/all_to_all | solution.py:49
  77.2 0.1 reduce_sum.19
  77.4 0.0 copy-start.4
  77.4 12.6 %all_gather.11 = f32[8,1,2,32,128]{4,3,2,1,0:T(8,128)S(1)} all-gather(f32[1,1,2,32,128]{4,3,2,1,0:T(8,128)S(1)} %copy.45), channel_id=1, replica_groups=mesh['row'=8,'col'=4] {'row'}, dimensions={0}, use_global_device_ids=true | all-gather | bytes 294912 | tf_op jit(solution)/shard_map/all_gather | solution.py:34
  90.0 0.0 copy-start.6
  90.0 4.7 %while.32 = (s32[]{:T(128)}, f32[2,32,128]{2,0,1:T(2,128)S(1)}, s32[]{:T(128)}, s32[16]{0:T(128)S(1)}, s32[]{:T(128)}, /*index=5*/s32[16]{0:T(128)S(1)}, f32[16,...) while((s32[]{:T(128)}, f32[2,32,128]{2,0,1:T(2,128)S(1)}, ...), condition=%wide.region_7.9_spmd, body=%wide.region_6.8_spmd.sunk | while | flops 51160188 | bytes 1250271 | solution.py:30
  90.1 0.7 compare_and_fusion.8
  90.8 0.6 gather_fusion.2
  91.4 0.6 fusion.84
  92.0 0.1 dynamic_slice.50
  92.0 0.3 convolution_add_fusion.8
  92.4 0.7 compare_and_fusion.8
  93.1 0.6 gather_fusion.2
  93.7 0.6 fusion.84
  94.3 0.1 dynamic_slice.50
  94.4 0.3 convolution_add_fusion.8
  94.8 0.3 fusion.44
  95.2 17.5 %psum.7 = f32[1,2,32,128]{3,2,1,0:T(8,128)} all-reduce(f32[1,2,32,128]{3,2,1,0:T(8,128)S(1)} %fusion.44), channel_id=1, replica_groups=mesh['row'=8,'col'=4] {'col'}, use_global_device_ids=true, to_apply=%region_8.10 | all-reduce | flops 8192 | bytes 65536 | tf_op jit(solution)/shard_map/psum | solution.py:99
  (30 shorter events, 0.3 us)
Async XLA Ops:
  0.6 1.5 %copy-start = (f32[1,1,2,128,128]{4,3,2,1,0:T(8,128)S(1)}, f32[1,1,2,128,128]{4,3,2,1,0:T(8,128)}, u32[]{:S(2)}) copy-start(f32[1,1,2,128,128]{4,3,2,1,0:T(8,128)} %param.21) | copy-start | bytes 393220
  13.1 24.6 %copy-start.2 = (f32[1,1,2,32,128]{4,3,2,1,0:T(8,128)S(1)}, f32[1,1,2,32,128]{4,3,2,1,0:T(8,128)}, u32[]{:S(2)}) copy-start(f32[1,1,2,32,128]{4,3,2,1,0:T(8,128)} %param.20) | copy-start | bytes 98308
  27.9 9.8 %all-to-all-start = ((f32[1,4,2,32,128]{4,2,3,0,1:T(2,128)}), f32[1,4,2,32,128]{4,2,3,0,1:T(2,128)S(1)}, u32[]{:S(2)}, u32[]{:S(2)}) async-start(f32[1,4,2,32,128]{4,2,3,0,1:T(2,128)} %copy.36), calls=%async_computation | async-start | bytes 262144 | tf_op jit(solution)/shard_map/all_to_all | solution.py:49
  38.0 15.1 %copy-start.3 = (f32[2,32,128]{2,1,0:T(8,128)}, f32[2,32,128]{2,1,0:T(8,128)S(1)}, u32[]{:S(2)}) copy-start(f32[2,32,128]{2,1,0:T(8,128)S(1)} %fusion.45) | copy-start | bytes 98308
  53.1 36.9 %copy-start.1 = (f32[1,1,16,128,128]{4,3,2,1,0:T(8,128)S(1)}, f32[1,1,16,128,128]{4,3,2,1,0:T(8,128)}, u32[]{:S(2)}) copy-start(f32[1,1,16,128,128]{4,3,2,1,0:T(8,128)} %param.26) | copy-start | bytes 3145732
  53.1 36.9 %copy-start.5 = (s32[1,1,16]{2,1,0:T(1,128)S(1)}, s32[1,1,16]{2,1,0:T(1,128)}, u32[]{:S(2)}) copy-start(s32[1,1,16]{2,1,0:T(1,128)} %param.28) | copy-start | bytes 196
  53.1 36.9 %copy-start.8 = (s32[1,1,16]{2,1,0:T(1,128)S(1)}, s32[1,1,16]{2,1,0:T(1,128)}, u32[]{:S(2)}) copy-start(s32[1,1,16]{2,1,0:T(1,128)} %param.27) | copy-start | bytes 196
  67.9 9.3 %all-to-all-start.1 = ((f32[1,4,2,32,128]{4,2,3,0,1:T(2,128)}), f32[1,4,2,32,128]{4,2,3,0,1:T(2,128)S(1)}, u32[]{:S(2)}, u32[]{:S(2)}) async-start(f32[1,4,2,32,128]{4,2,3,0,1:T(2,128)} %copy.40), calls=%async_computation.1 | async-start | bytes 262144 | tf_op jit(solution)/shard_map/all_to_all | solution.py:49
  77.4 12.7 %copy-start.4 = (f32[1,1,2,32,128]{4,3,2,1,0:T(8,128)}, f32[1,1,2,32,128]{4,3,2,1,0:T(8,128)S(1)}, u32[]{:S(2)}) copy-start(f32[1,1,2,32,128]{4,3,2,1,0:T(8,128)S(1)} %copy.45) | copy-start | bytes 98308
  90.0 4.7 %copy-start.6 = (f32[1,1,2,128]{3,2,1,0:T(2,128)S(1)}, f32[1,1,2,128]{3,2,1,0:T(2,128)}, u32[]{:S(2)}) copy-start(f32[1,1,2,128]{3,2,1,0:T(2,128)} %param.30) | copy-start | bytes 3076
  90.0 4.8 %copy-start.7 = (s32[1,1,2,128]{3,2,1,0:T(2,128)S(1)}, s32[1,1,2,128]{3,2,1,0:T(2,128)}, u32[]{:S(2)}) copy-start(s32[1,1,2,128]{3,2,1,0:T(2,128)} %param.31) | copy-start | bytes 3076
where the time goes:
time: 114 us; the launch traced here: 113 us
  blocking collectives  55.8 us (49%)
  matrix products  14.5 us (13%)
  local copies, waits for them, and re-layouts  11.3 us (10%)
  waiting for transfers between devices  11.2 us (10%)
  other arithmetic  10.1 us (9%)
  starting transfers between devices  7.17 us (6%)
  between operations  2.25 us (2%)
    all_gather x3, blocking collectives, gather_columns(): whole = lax.all_gather(vec[None, None], 'row', axis=0, tiled=True)  38.4 us
    psum x1, blocking collectives, body(): coarse = lax.psum(part, 'col')  17.5 us
    all_to_all x2, waiting for transfers between devices, stiffness_product(): lax.all_to_all(partial_value, 'col', split_axis=1, concat_axis=0, tiled=T...  11.2 us
    dot_general x8, matrix products, add_group(): product = jnp.einsum('ska,sab->skb', inputs, piece, precision=highest)  11.1 us
    and x8, other arithmetic, add_group(): inputs = jnp.take(blocks, col_ids, axis=0)  9.83 us
    all_to_all x2, starting transfers between devices, stiffness_product(): lax.all_to_all(partial_value, 'col', split_axis=1, concat_axis=0, tiled=T...  7.17 us
    dynamic_slice x8, local copies, waits for them, and re-layouts, add_group(): row_ids = lax.dynamic_slice_in_dim(rows, start, tile_group, 0)  4.52 us
    gather x8, local copies, waits for them, and re-layouts, add_group(): inputs = jnp.take(blocks, col_ids, axis=0)  4.45 us
  transfers between devices with their start and end apart: 2, of which 2 were waited for; matrix products, arithmetic and copies ran while one was open for 0% of the time, Pallas kernels for 0%

commit v1 on v0

v1 whole, which is shorter than its diff:
```python
import functools

import jax
import jax.numpy as jnp
from jax import lax
from jax.experimental import pallas as pl
from jax.experimental.pallas import tpu as pltpu
from jax.sharding import PartitionSpec as P

omega = 0.7
MESH = pl.DeviceIdType.MESH
f32, bf16 = jnp.float32, jnp.bfloat16
unrolled_most = 8
slot_group = 8


def loop(low, high, step):
    if high - low <= unrolled_most:
        for index in range(low, high):
            step(index)
    else:

        def one(index, carry):
            step(index)
            return carry

        lax.fori_loop(low, high, one, 0)


def split(value):
    high = value.astype(bf16)
    low = (value - high.astype(f32)).astype(bf16)
    return high, low


def wide(value):
    return jnp.concatenate(split(value), axis=-1)


def times(left, weight):
    both = jnp.dot(left, weight, preferred_element_type=f32)
    half = both.shape[-1] // 2
    return both[:, :half] + both[:, half:]


def kernel(
    nr, nc,
    f_hbm, d_hbm, a_hbm, src_s, tgt_s, cnt_s, b_hbm, clu_s, btgt_s, bcnt_s, w_ref, lab_ref,
    x_out, r_out, c_out,
    f_v, d_v, a_v, b_v, wd, wa, wb, gath, xs, prod, part, pieces, coarse_v, onehot,
    x_v, c_v, live_a, live_b,
    in_sem, a_sem, out_sem, rsend, rrecv, csend, crecv,
):
    pb, nrhs, blk = f_v.shape
    slots, bslots = a_v.shape[0], b_v.shape[0]
    chunks = a_sem.shape[0]
    per = slots // chunks
    row, col = lax.axis_index("row"), lax.axis_index("col")

    f_in = pltpu.make_async_copy(f_hbm.at[0, 0], f_v, in_sem.at[0])
    d_in = pltpu.make_async_copy(d_hbm.at[0, 0], d_v, in_sem.at[1])
    b_in = pltpu.make_async_copy(b_hbm.at[0, 0], b_v, in_sem.at[2])
    a_in = [
        pltpu.make_async_copy(a_hbm.at[0, 0, pl.ds(c * per, per)], a_v.at[pl.ds(c * per, per)], a_sem.at[c])
        for c in range(chunks)
    ]
    d_in.start()
    f_in.start()
    for copy in a_in:
        copy.start()
    b_in.start()

    barrier = pltpu.get_barrier_semaphore()

    def greet_row(k):
        pl.semaphore_signal(barrier, inc=1, device_id={"row": lax.rem(row + k, nr)}, device_id_type=MESH)

    def greet_col(k):
        pl.semaphore_signal(barrier, inc=1, device_id={"col": lax.rem(col + k, nc)}, device_id_type=MESH)

    loop(1, nr, greet_row)
    loop(1, nc, greet_col)

    def row_copy(phase, k, owner):
        return pltpu.make_async_remote_copy(
            src_ref=gath.at[phase, owner],
            dst_ref=gath.at[phase, owner],
            send_sem=rsend.at[phase, k],
            recv_sem=rrecv.at[phase, k],
            device_id={"row": lax.rem(row + k, nr)},
            device_id_type=MESH,
        )

    def spread(phase):
        loop(1, nr, lambda k: row_copy(phase, k, row).start())

    def collect(phase):
        def take(owner):
            for p in range(pb):
                xs[owner * pb + p] = wide(gath[phase, owner, p])

        take(row)

        def arrive(k):
            owner = lax.rem(row + nr - k, nr)
            row_copy(phase, k, owner).wait_recv()
            take(owner)

        loop(1, nr, arrive)

    def piece_copy(phase, k, owner, source):
        return pltpu.make_async_remote_copy(
            src_ref=part.at[phase, owner],
            dst_ref=pieces.at[phase, source],
            send_sem=csend.at[phase, k],
            recv_sem=crecv.at[phase, k],
            device_id={"col": lax.rem(col + k, nc)},
            device_id_type=MESH,
        )

    def prepare(weight, k, tile):
        both = wide(tile)
        weight[k, :blk] = both
        weight[k, blk:] = both

    def products(weight, target, count):
        def group(index, carry):
            for j in range(slot_group):
                s = index * slot_group + j
                prod[s] = times(xs[target[0, 0, s]], weight[s])
            return carry

        lax.fori_loop(0, count // slot_group, group, 0)

    def chosen(live, count, block):
        total = jnp.zeros((nrhs, blk), f32)
        for s in range(count):
            total = total + jnp.where(live[s] == block, prod[s], 0.0)
        return total

    def operator(phase):
        collect(phase)
        products(wa, tgt_s, slots)

        def piece(k):
            owner = lax.rem(col + k, nc)
            for p in range(pb):
                part[phase, owner, p] = chosen(live_a, slots, owner * pb + p)
            piece_copy(phase, k, owner, col).start()

        loop(1, nc, piece)
        image = [chosen(live_a, slots, col * pb + p) for p in range(pb)]
        for p in range(pb):
            pieces[phase, col, p] = image[p]

        def arrive(k):
            source = lax.rem(col + nc - k, nc)
            piece_copy(phase, k, col, source).wait_recv()

        loop(1, nc, arrive)
        return [jnp.sum(pieces[phase, :, p], axis=0) for p in range(pb)]

    d_in.wait()
    for p in range(pb):
        prepare(wd, p, d_v[p])
    f_in.wait()
    for p in range(pb):
        gath[0, row, p] = omega * times(wide(f_v[p]), wd[p])
    pl.semaphore_wait(barrier, nr + nc - 2)
    spread(0)

    for c in range(chunks):
        a_in[c].wait()

        def prepare_a(j, carry):
            prepare(wa, c * per + j, a_v[c * per + j])
            return carry

        lax.fori_loop(0, per, prepare_a, 0)

    def keep_a(s, carry):
        live_a[s] = jnp.where(s < cnt_s[0, 0], src_s[0, 0, s], -1)
        return carry

    lax.fori_loop(0, slots, keep_a, 0)

    image = operator(0)
    for p in range(pb):
        x = gath[0, row, p] + omega * times(wide(f_v[p] - image[p]), wd[p])
        gath[1, row, p] = x
        x_v[p] = x
    spread(1)
    x_copy = pltpu.make_async_copy(x_v, x_out.at[0, 0], out_sem.at[0])
    x_copy.start()

    b_in.wait()

    def prepare_b(j, carry):
        prepare(wb, j, b_v[j])
        return carry

    lax.fori_loop(0, bslots, prepare_b, 0)

    def keep_b(s, carry):
        live_b[s] = jnp.where(s < bcnt_s[0, 0], clu_s[0, 0, s], -1)
        return carry

    lax.fori_loop(0, bslots, keep_b, 0)
    aggregate = lax.broadcasted_iota(jnp.int32, (pb * blk, blk), 0)
    for p in range(pb):
        same = aggregate == lab_ref[0, 0, p : p + 1, :]
        onehot[:, p * blk : (p + 1) * blk] = jnp.where(same, 1.0, 0.0).astype(bf16)

    image = operator(1)
    for p in range(pb):
        gath[2, row, p] = f_v[p] - image[p]
    spread(2)
    r_copy = pltpu.make_async_copy(gath.at[2, row], r_out.at[0, 0], out_sem.at[1])
    r_copy.start()

    weighted = jnp.concatenate(
        [gath[2, row, p] * w_ref[0, 0, p : p + 1, :] for p in range(pb)], axis=-1
    )
    contract = functools.partial(
        lax.dot_general,
        dimension_numbers=(((1,), (1,)), ((), ())),
        preferred_element_type=f32,
    )
    high, low = split(weighted)
    tentative = contract(high, onehot[...]) + contract(low, onehot[...])
    for p in range(pb):
        c_v[p] = tentative[:, p * blk : (p + 1) * blk]

    collect(2)
    products(wb, btgt_s, bslots)
    for p in range(pb):
        coarse_v[col, p] = c_v[p] + chosen(live_b, bslots, p)

    def coarse_copy(k, source):
        return pltpu.make_async_remote_copy(
            src_ref=coarse_v.at[source],
            dst_ref=coarse_v.at[source],
            send_sem=csend.at[2, k],
            recv_sem=crecv.at[2, k],
            device_id={"col": lax.rem(col + k, nc)},
            device_id_type=MESH,
        )

    loop(1, nc, lambda k: coarse_copy(k, col).start())
    loop(1, nc, lambda k: coarse_copy(k, lax.rem(col + nc - k, nc)).wait_recv())
    for p in range(pb):
        c_v[p] = jnp.sum(coarse_v[:, p], axis=0)
    c_copy = pltpu.make_async_copy(c_v, c_out.at[0], out_sem.at[2])
    c_copy.start()

    for phase in range(3):
        loop(1, nr, lambda k: row_copy(phase, k, row).wait_send())
    for phase in range(2):
        loop(1, nc, lambda k: piece_copy(phase, k, lax.rem(col + k, nc), col).wait_send())
    loop(1, nc, lambda k: coarse_copy(k, col).wait_send())
    x_copy.wait()
    r_copy.wait()
    c_copy.wait()


def body(nr, nc, *args):
    f, d, a, src, tgt, cnt, b, clu, btgt, bcnt, w, lab = args
    pb, nrhs, blk = f.shape[2:]
    slots, bslots = a.shape[2], b.shape[2]
    chunks = 4
    anyspace = pl.BlockSpec(memory_space=pl.ANY)
    smem = pl.BlockSpec(memory_space=pltpu.SMEM)
    vmem = pl.BlockSpec(memory_space=pltpu.VMEM)
    block = (pb, nrhs, blk)
    dma = pltpu.SemaphoreType.DMA
    flops = 8 * (2 * slots + bslots + 3 * pb) * nrhs * blk * blk
    return pl.pallas_call(
        functools.partial(kernel, nr, nc),
        out_shape=(
            jax.ShapeDtypeStruct(f.shape, f32),
            jax.ShapeDtypeStruct(f.shape, f32),
            jax.ShapeDtypeStruct((1,) + block, f32),
        ),
        in_specs=[anyspace, anyspace, anyspace, smem, smem, smem, anyspace, smem, smem, smem, vmem, vmem],
        out_specs=(anyspace, anyspace, anyspace),
        scratch_shapes=[
            pltpu.VMEM(block, f32),
            pltpu.VMEM((pb, blk, blk), f32),
            pltpu.VMEM((slots, blk, blk), f32),
            pltpu.VMEM((bslots, blk, blk), f32),
            pltpu.VMEM((pb, 2 * blk, 2 * blk), bf16),
            pltpu.VMEM((slots, 2 * blk, 2 * blk), bf16),
            pltpu.VMEM((bslots, 2 * blk, 2 * blk), bf16),
            pltpu.VMEM((3, nr) + block, f32),
            pltpu.VMEM((nr * pb, nrhs, 2 * blk), bf16),
            pltpu.VMEM((slots, nrhs, blk), f32),
            pltpu.VMEM((2, nc) + block, f32),
            pltpu.VMEM((2, nc) + block, f32),
            pltpu.VMEM((nc,) + block, f32),
            pltpu.VMEM((pb * blk, pb * blk), bf16),
            pltpu.VMEM(block, f32),
            pltpu.VMEM(block, f32),
            pltpu.SMEM((slots,), jnp.int32),
            pltpu.SMEM((bslots,), jnp.int32),
            dma((3,)),
            dma((chunks,)),
            dma((3,)),
            dma((3, nr)),
            dma((3, nr)),
            dma((3, nc)),
            dma((3, nc)),
        ],
        compiler_params=pltpu.CompilerParams(
            collective_id=0, has_side_effects=True, vmem_limit_bytes=40 * 1024 * 1024
        ),
        cost_estimate=pl.CostEstimate(
            flops=flops, bytes_accessed=4 * blk * blk * (slots + bslots + pb), transcendentals=0
        ),
    )(f, d, a, src, tgt, cnt, b, clu, btgt, bcnt, w, lab)


def solution(mesh):
    tensor = P("row", "col", None, None, None)
    index = P("row", "col", None)
    plain = P("row", "col", None, None)
    tally = P("row", "col")
    return jax.shard_map(
        functools.partial(body, mesh.shape["row"], mesh.shape["col"]),
        mesh=mesh,
        in_specs=(tensor, tensor, tensor, index, index, tally, tensor, index, index, tally, plain, plain),
        out_specs=(tensor, tensor, P("row", None, None, None)),
        check_vma=False,
    )
```

time: 114 us -> 50.3 us (0.44)
  blocking collectives: 55.8 us -> 0 us
  Pallas kernels: 0 us -> 37.7 us
  matrix products: 14.5 us -> 0 us
  waiting for transfers between devices: 11.2 us -> 0 us
  other arithmetic: 10.1 us -> 0 us
  starting transfers between devices: 7.17 us -> 0 us
    all_gather x3 -> x0, blocking collectives: 38.4 us -> none  [gather_columns(): whole = lax.all_gather(vec[None, None], 'row', axis=0, tiled=True)]
    pallas_call x0 -> x1, Pallas kernels: none -> 37.7 us  [body(): pl.pallas_call(functools.partial(kernel, nr, nc), out_shape=(jax.ShapeDty...]
    psum x1 -> x0, blocking collectives: 17.5 us -> none  [body(): coarse = lax.psum(part, 'col')]
    dot_general x19 -> x0, matrix products: 14.5 us -> none  [the longest x8 11.1 us: add_group(): product = jnp.einsum('ska,sab->skb', inputs, piece, precision=highest)]
    all_to_all x2 -> x0, waiting for transfers between devices: 11.2 us -> none  [stiffness_product(): lax.all_to_all(partial_value, 'col', split_axis=1, concat_axis=0, tiled=T...]
    and x8 -> x0, other arithmetic: 9.83 us -> none  [add_group(): inputs = jnp.take(blocks, col_ids, axis=0)]
    unnamed x20 -> x23, local copies, waits for them, and re-layouts: 0.85 us -> 10.3 us
    all_to_all x2 -> x0, starting transfers between devices: 7.17 us -> none  [stiffness_product(): lax.all_to_all(partial_value, 'col', split_axis=1, concat_axis=0, tiled=T...]
  transfers between devices with their start and end apart: 2 -> 0, of which waited for: 2 -> 0; matrix products, arithmetic and copies ran while one was open for 0% -> 0% of each run, Pallas kernels for 0% -> 0%
where the time goes in v1:
time: 50.3 us; the launch traced here: 49.9 us
  Pallas kernels  37.7 us (75%)
  local copies, waits for them, and re-layouts  10.3 us (20%)
  between operations  1.95 us (4%)
    pallas_call x1, Pallas kernels, body(): pl.pallas_call(functools.partial(kernel, nr, nc), out_shape=(jax.ShapeDty...  37.7 us
    unnamed x23, local copies, waits for them, and re-layouts  10.3 us

profile of v1, /device:TPU:0, one launch (start us, length us, event | category | flops | bytes accessed | tf_op | source)
XLA Modules:
  0.0 49.9 jit_solution(11364394954038674859)
XLA Ops:
  1.9 0.0 copy-start
  1.9 1.6 %copy-done = f32[1,1,32,128,128]{4,3,2,1,0:T(8,128)S(1)} copy-done((f32[1,1,32,128,128]{4,3,2,1,0:T(8,128)S(1)}, f32[1,1,32,128,128]{4,3,2,1,0:T(8,128)}, u32[]{:S(2)}) %copy-start) | copy-done | bytes 2097176
  3.5 0.0 copy-start.1
  3.5 1.2 %copy-done.1 = f32[1,1,16,128,128]{4,3,2,1,0:T(8,128)S(1)} copy-done((f32[1,1,16,128,128]{4,3,2,1,0:T(8,128)S(1)}, f32[1,1,16,128,128]{4,3,2,1,0:T(8,128)}, u32[]{:S(2)}) %copy-start.1) | copy-done | bytes 1048600
  4.7 0.0 copy-start.2
  4.7 0.9 %copy-done.2 = f32[1,1,2,128,128]{4,3,2,1,0:T(8,128)S(1)} copy-done((f32[1,1,2,128,128]{4,3,2,1,0:T(8,128)S(1)}, f32[1,1,2,128,128]{4,3,2,1,0:T(8,128)}, u32[]{:S(2)}) %copy-start.2) | copy-done | bytes 131096
  5.6 0.0 copy-start.3
  5.7 0.8 %copy-done.3 = f32[1,1,2,32,128]{4,3,2,1,0:T(8,128)S(1)} copy-done((f32[1,1,2,32,128]{4,3,2,1,0:T(8,128)S(1)}, f32[1,1,2,32,128]{4,3,2,1,0:T(8,128)}, u32[]{:S(2)}) %copy-start.3) | copy-done | bytes 32792
  6.4 0.0 copy-start.4
  6.4 0.7 %copy-done.4 = f32[1,1,2,128]{3,2,1,0:T(2,128)S(1)} copy-done((f32[1,1,2,128]{3,2,1,0:T(2,128)S(1)}, f32[1,1,2,128]{3,2,1,0:T(2,128)}, u32[]{:S(2)}) %copy-start.4) | copy-done | bytes 1048
  7.1 0.0 copy-start.5
  7.1 0.7 %copy-done.5 = s32[1,1,2,128]{3,2,1,0:T(2,128)S(1)} copy-done((s32[1,1,2,128]{3,2,1,0:T(2,128)S(1)}, s32[1,1,2,128]{3,2,1,0:T(2,128)}, u32[]{:S(2)}) %copy-start.5) | copy-done | bytes 1048
  7.8 0.0 copy-start.6
  7.8 0.7 %copy-done.6 = s32[1,1,32]{2,1,0:T(1,128)S(1)} copy-done((s32[1,1,32]{2,1,0:T(1,128)S(1)}, s32[1,1,32]{2,1,0:T(1,128)}, u32[]{:S(2)}) %copy-start.6) | copy-done | bytes 152
  8.4 0.0 copy-start.7
  8.4 0.7 %copy-done.7 = s32[1,1,32]{2,1,0:T(1,128)S(1)} copy-done((s32[1,1,32]{2,1,0:T(1,128)S(1)}, s32[1,1,32]{2,1,0:T(1,128)}, u32[]{:S(2)}) %copy-start.7) | copy-done | bytes 152
  9.1 0.0 copy-start.8
  9.1 0.7 %copy-done.8 = s32[1,1,16]{2,1,0:T(1,128)S(1)} copy-done((s32[1,1,16]{2,1,0:T(1,128)S(1)}, s32[1,1,16]{2,1,0:T(1,128)}, u32[]{:S(2)}) %copy-start.8) | copy-done | bytes 88
  9.7 0.0 copy-start.9
  9.7 0.7 %copy-done.9 = s32[1,1,16]{2,1,0:T(1,128)S(1)} copy-done((s32[1,1,16]{2,1,0:T(1,128)S(1)}, s32[1,1,16]{2,1,0:T(1,128)}, u32[]{:S(2)}) %copy-start.9) | copy-done | bytes 88
  10.4 37.7 %shard_map.139 = (f32[1,1,2,32,128]{4,3,2,1,0:T(8,128)S(1)}, f32[1,1,2,32,128]{4,3,2,1,0:T(8,128)S(1)}, f32[1,2,32,128]{3,2,1,0:T(8,128)S(1)}) custom-call(f32[1,1,2,32,128]{4,3,2,1,0:T(8,128)S(1)} %copy-done.3, f32[1,1,2,128,128]{4,3,2,1,0:T(8,128)S(1)} %copy-done.2, f32[1,1,32,128,128]{4,3,2,1,0:T(8,128)S(1)} %copy-done, s32[1,1,32]{2,1,0:T(1,128)S(1)} %copy-done.6, ...), custom_call_target="tpu_custom_call" | custom-call | flops 360710144 | bytes 3276800 | tf_op jit(solution)/shard_map/pallas_call | solution.py:277
  48.1 0.6 %copy.20 = f32[1,1,2,32,128]{4,3,2,1,0:T(8,128)} copy(f32[1,1,2,32,128]{4,3,2,1,0:T(8,128)S(1)} %get-tuple-element.6) | data formatting | bytes 65536
  48.7 0.6 %copy.21 = f32[1,1,2,32,128]{4,3,2,1,0:T(8,128)} copy(f32[1,1,2,32,128]{4,3,2,1,0:T(8,128)S(1)} %get-tuple-element.7) | data formatting | bytes 65536
  49.3 0.6 %copy.22 = f32[1,2,32,128]{3,2,1,0:T(8,128)} copy(f32[1,2,32,128]{3,2,1,0:T(8,128)S(1)} %get-tuple-element.8) | data formatting | bytes 65536
Async XLA Ops:
  1.9 1.6 %copy-start = (f32[1,1,32,128,128]{4,3,2,1,0:T(8,128)S(1)}, f32[1,1,32,128,128]{4,3,2,1,0:T(8,128)}, u32[]{:S(2)}) copy-start(f32[1,1,32,128,128]{4,3,2,1,0:T(8,128)} %a_hbm.1) | copy-start | bytes 6291460
  3.5 1.2 %copy-start.1 = (f32[1,1,16,128,128]{4,3,2,1,0:T(8,128)S(1)}, f32[1,1,16,128,128]{4,3,2,1,0:T(8,128)}, u32[]{:S(2)}) copy-start(f32[1,1,16,128,128]{4,3,2,1,0:T(8,128)} %b_hbm.1) | copy-start | bytes 3145732
  4.7 0.9 %copy-start.2 = (f32[1,1,2,128,128]{4,3,2,1,0:T(8,128)S(1)}, f32[1,1,2,128,128]{4,3,2,1,0:T(8,128)}, u32[]{:S(2)}) copy-start(f32[1,1,2,128,128]{4,3,2,1,0:T(8,128)} %d_hbm.1) | copy-start | bytes 393220
  5.6 0.8 %copy-start.3 = (f32[1,1,2,32,128]{4,3,2,1,0:T(8,128)S(1)}, f32[1,1,2,32,128]{4,3,2,1,0:T(8,128)}, u32[]{:S(2)}) copy-start(f32[1,1,2,32,128]{4,3,2,1,0:T(8,128)} %f_hbm.1) | copy-start | bytes 98308
  6.4 0.7 %copy-start.4 = (f32[1,1,2,128]{3,2,1,0:T(2,128)S(1)}, f32[1,1,2,128]{3,2,1,0:T(2,128)}, u32[]{:S(2)}) copy-start(f32[1,1,2,128]{3,2,1,0:T(2,128)} %w_ref.1) | copy-start | bytes 3076
  7.1 0.7 %copy-start.5 = (s32[1,1,2,128]{3,2,1,0:T(2,128)S(1)}, s32[1,1,2,128]{3,2,1,0:T(2,128)}, u32[]{:S(2)}) copy-start(s32[1,1,2,128]{3,2,1,0:T(2,128)} %lab_ref.1) | copy-start | bytes 3076
  7.8 0.7 %copy-start.6 = (s32[1,1,32]{2,1,0:T(1,128)S(1)}, s32[1,1,32]{2,1,0:T(1,128)}, u32[]{:S(2)}) copy-start(s32[1,1,32]{2,1,0:T(1,128)} %src_s.1) | copy-start | bytes 388
  8.4 0.7 %copy-start.7 = (s32[1,1,32]{2,1,0:T(1,128)S(1)}, s32[1,1,32]{2,1,0:T(1,128)}, u32[]{:S(2)}) copy-start(s32[1,1,32]{2,1,0:T(1,128)} %tgt_s.1) | copy-start | bytes 388
  9.1 0.7 %copy-start.8 = (s32[1,1,16]{2,1,0:T(1,128)S(1)}, s32[1,1,16]{2,1,0:T(1,128)}, u32[]{:S(2)}) copy-start(s32[1,1,16]{2,1,0:T(1,128)} %clu_s.1) | copy-start | bytes 196
  9.7 0.7 %copy-start.9 = (s32[1,1,16]{2,1,0:T(1,128)S(1)}, s32[1,1,16]{2,1,0:T(1,128)}, u32[]{:S(2)}) copy-start(s32[1,1,16]{2,1,0:T(1,128)} %btgt_s.1) | copy-start | bytes 196

commit v2 on v1

v2 whole, which is shorter than its diff:
```python
import functools

import jax
import jax.numpy as jnp
from jax import lax
from jax.experimental import pallas as pl
from jax.experimental.pallas import tpu as pltpu
from jax.sharding import PartitionSpec as P

omega = 0.7
MESH = pl.DeviceIdType.MESH
f32, bf16 = jnp.float32, jnp.bfloat16
unrolled_most = 8
slot_group = 8
vmem_bytes = 60 * 1024 * 1024
halves = 2


def loop(low, high, step):
    if high - low <= unrolled_most:
        for index in range(low, high):
            step(index)
    else:

        def one(index, carry):
            step(index)
            return carry

        lax.fori_loop(low, high, one, 0)


def split(value):
    high = value.astype(bf16)
    low = (value - high.astype(f32)).astype(bf16)
    return high, low


def wide(value):
    return jnp.concatenate(split(value), axis=-1)


def times(left, weight):
    both = jnp.dot(left, weight, preferred_element_type=f32)
    half = both.shape[-1] // 2
    return both[:, :half] + both[:, half:]


def kernel(
    nr, nc, parts,
    f_hbm, d_hbm, a_hbm, src_h, tgt_h, cnt_s, b_hbm, clu_h, btgt_h, bcnt_s, w_h, lab_h,
    x_out, r_out, c_out,
    f_v, d_v, a_v, b_v, wd, wa, wb, gath, xs, prod, part, pieces, coarse_v, onehot,
    x_v, r_v, c_v, live_a, live_b, src_s, tgt_s, clu_s, btgt_s, w_ref, lab_ref,
    in_sem, small_sem, a_sem, out_sem, rsend, rrecv, csend, crecv,
):
    pb, nrhs, blk = f_v.shape
    some = nrhs // parts
    slots, bslots = a_v.shape[0], b_v.shape[0]
    chunks = a_sem.shape[0]
    per = slots // chunks
    row, col = lax.axis_index("row"), lax.axis_index("col")

    d_in = pltpu.make_async_copy(d_hbm.at[0, 0], d_v, in_sem.at[0])
    f_in = pltpu.make_async_copy(f_hbm.at[0, 0], f_v, in_sem.at[1])
    b_in = pltpu.make_async_copy(b_hbm.at[0, 0], b_v, in_sem.at[2])
    a_in = [
        pltpu.make_async_copy(a_hbm.at[0, 0, pl.ds(c * per, per)], a_v.at[pl.ds(c * per, per)], a_sem.at[c])
        for c in range(chunks)
    ]
    small = [
        pltpu.make_async_copy(source, held, small_sem.at[i])
        for i, (source, held) in enumerate(
            ((tgt_h, tgt_s), (src_h, src_s), (btgt_h, btgt_s), (clu_h, clu_s), (w_h, w_ref), (lab_h, lab_ref))
        )
    ]
    d_in.start()
    f_in.start()

    barrier = pltpu.get_barrier_semaphore()

    def greet_row(k):
        pl.semaphore_signal(barrier, inc=1, device_id={"row": lax.rem(row + k, nr)}, device_id_type=MESH)

    def greet_col(k):
        pl.semaphore_signal(barrier, inc=1, device_id={"col": lax.rem(col + k, nc)}, device_id_type=MESH)

    loop(1, nr, greet_row)
    loop(1, nc, greet_col)
    for copy in a_in:
        copy.start()
    for copy in small:
        copy.start()
    b_in.start()

    def rows_of(h):
        return slice(h * some, (h + 1) * some)

    def row_copy(phase, h, k, owner):
        return pltpu.make_async_remote_copy(
            src_ref=gath.at[phase, h, owner],
            dst_ref=gath.at[phase, h, owner],
            send_sem=rsend.at[phase, h, k],
            recv_sem=rrecv.at[phase, h, k],
            device_id={"row": lax.rem(row + k, nr)},
            device_id_type=MESH,
        )

    def spread(phase, h):
        loop(1, nr, lambda k: row_copy(phase, h, k, row).start())

    def collect(phase, h):
        def take(owner):
            for p in range(pb):
                xs[owner * pb + p] = wide(gath[phase, h, owner, p])

        take(row)

        def arrive(k):
            owner = lax.rem(row + nr - k, nr)
            row_copy(phase, h, k, owner).wait_recv()
            take(owner)

        loop(1, nr, arrive)

    def piece_copy(phase, h, k, owner, source):
        return pltpu.make_async_remote_copy(
            src_ref=part.at[phase, h, owner],
            dst_ref=pieces.at[phase, h, source],
            send_sem=csend.at[phase, h, k],
            recv_sem=crecv.at[phase, h, k],
            device_id={"col": lax.rem(col + k, nc)},
            device_id_type=MESH,
        )

    def coarse_copy(h, k, source):
        return pltpu.make_async_remote_copy(
            src_ref=coarse_v.at[h, source],
            dst_ref=coarse_v.at[h, source],
            send_sem=csend.at[2, h, k],
            recv_sem=crecv.at[2, h, k],
            device_id={"col": lax.rem(col + k, nc)},
            device_id_type=MESH,
        )

    def source_of(k):
        return lax.rem(col + nc - k, nc)

    def prepare(weight, k, tile):
        both = wide(tile)
        weight[k, :blk] = both
        weight[k, blk:] = both

    def products(weight, target, count):
        def group(index, carry):
            for j in range(slot_group):
                s = index * slot_group + j
                prod[s] = times(xs[target[0, 0, s]], weight[s])
            return carry

        lax.fori_loop(0, count // slot_group, group, 0)

    def chosen(live, count, first):
        totals = [jnp.zeros((some, blk), f32) for p in range(pb)]
        for s in range(count):
            held, block = prod[s], live[s] - first
            totals = [total + jnp.where(block == p, held, 0.0) for p, total in enumerate(totals)]
        return totals

    def forward(phase, h):
        collect(phase, h)
        products(wa, tgt_s, slots)

        def piece(k, carry):
            owner = lax.rem(col + k, nc)
            for p, total in enumerate(chosen(live_a, slots, owner * pb)):
                part[phase, h, owner, p] = total

            @pl.when(k < nc)
            def _():
                piece_copy(phase, h, k, owner, col).start()

            return carry

        lax.fori_loop(1, nc + 1, piece, 0)

    def both(step):
        def one(h, carry):
            step(h)
            return carry

        lax.fori_loop(0, parts, one, 0)

    def image(phase, h):
        loop(1, nc, lambda k: piece_copy(phase, h, k, col, source_of(k)).wait_recv())
        totals = [part[phase, h, col, p] for p in range(pb)]
        for k in range(1, nc):
            totals = [total + pieces[phase, h, source_of(k), p] for p, total in enumerate(totals)]
        return totals

    d_in.wait()
    for p in range(pb):
        prepare(wd, p, d_v[p])
    f_in.wait()
    for p in range(pb):
        x = omega * times(wide(f_v[p]), wd[p])
        for h in range(parts):
            gath[0, h, row, p] = x[rows_of(h)]
    pl.semaphore_wait(barrier, nr + nc - 2)
    for h in range(parts):
        spread(0, h)

    for c in range(chunks):
        a_in[c].wait()

        def prepare_a(j, carry):
            prepare(wa, c * per + 2 * j, a_v[c * per + 2 * j])
            prepare(wa, c * per + 2 * j + 1, a_v[c * per + 2 * j + 1])
            return carry

        lax.fori_loop(0, per // 2, prepare_a, 0)

    for copy in small:
        copy.wait()

    def keep_a(s, carry):
        live_a[s] = jnp.where(s < cnt_s[0, 0], src_s[0, 0, s], -1)
        return carry

    lax.fori_loop(0, slots, keep_a, 0)

    both(lambda h: forward(0, h))

    b_in.wait()

    def prepare_b(j, carry):
        prepare(wb, j, b_v[j])
        return carry

    def keep_b(s, carry):
        live_b[s] = jnp.where(s < bcnt_s[0, 0], clu_s[0, 0, s], -1)
        return carry

    for h in range(parts):
        total = image(0, h)
        for p in range(pb):
            right = f_v[p, rows_of(h)] - total[p]
            x = gath[0, h, row, p] + omega * times(wide(right), wd[p])
            gath[1, h, row, p] = x
            x_v[p, rows_of(h)] = x
        spread(1, h)
    x_copy = pltpu.make_async_copy(x_v, x_out.at[0, 0], out_sem.at[0])
    x_copy.start()

    lax.fori_loop(0, bslots, prepare_b, 0)
    lax.fori_loop(0, bslots, keep_b, 0)
    aggregate = lax.broadcasted_iota(jnp.int32, (pb * blk, blk), 0)
    for p in range(pb):
        same = aggregate == lab_ref[0, 0, p : p + 1, :]
        onehot[:, p * blk : (p + 1) * blk] = jnp.where(same, 1.0, 0.0).astype(bf16)

    both(lambda h: forward(1, h))
    for h in range(parts):
        total = image(1, h)
        for p in range(pb):
            left = f_v[p, rows_of(h)] - total[p]
            gath[2, h, row, p] = left
            r_v[p, rows_of(h)] = left
        spread(2, h)
    r_copy = pltpu.make_async_copy(r_v, r_out.at[0, 0], out_sem.at[1])
    r_copy.start()

    weighted = jnp.concatenate([r_v[p] * w_ref[0, 0, p : p + 1, :] for p in range(pb)], axis=-1)
    contract = functools.partial(
        lax.dot_general,
        dimension_numbers=(((1,), (1,)), ((), ())),
        preferred_element_type=f32,
    )
    high, low = split(weighted)
    tentative = contract(high, onehot[...]) + contract(low, onehot[...])
    for p in range(pb):
        for h in range(parts):
            coarse_v[h, col, p] = tentative[rows_of(h), p * blk : (p + 1) * blk]

    def restrict(h):
        collect(2, h)
        products(wb, btgt_s, bslots)
        for p, total in enumerate(chosen(live_b, bslots, 0)):
            coarse_v[h, col, p] = coarse_v[h, col, p] + total
        loop(1, nc, lambda k: coarse_copy(h, k, col).start())

    both(restrict)

    for phase in range(3):
        for h in range(parts):
            loop(1, nr, lambda k: row_copy(phase, h, k, row).wait_send())
    for phase in range(2):
        for h in range(parts):
            loop(1, nc, lambda k: piece_copy(phase, h, k, lax.rem(col + k, nc), col).wait_send())
    x_copy.wait()
    r_copy.wait()
    for h in range(parts):
        loop(1, nc, lambda k: coarse_copy(h, k, source_of(k)).wait_recv())
        for p in range(pb):
            c_v[p, rows_of(h)] = jnp.sum(coarse_v[h, :, p], axis=0)
    c_copy = pltpu.make_async_copy(c_v, c_out.at[0], out_sem.at[2])
    c_copy.start()
    for h in range(parts):
        loop(1, nc, lambda k: coarse_copy(h, k, col).wait_send())
    c_copy.wait()


def body(nr, nc, *args):
    f, d, a, src, tgt, cnt, b, clu, btgt, bcnt, w, lab = args
    pb, nrhs, blk = f.shape[2:]
    slots, bslots = a.shape[2], b.shape[2]
    chunks = 4
    parts = halves
    some = (pb, nrhs // parts, blk)
    anyspace = pl.BlockSpec(memory_space=pl.ANY)
    smem = pl.BlockSpec(memory_space=pltpu.SMEM)
    block = (pb, nrhs, blk)
    dma = pltpu.SemaphoreType.DMA
    flops = 8 * (2 * slots + bslots + 3 * pb) * nrhs * blk * blk
    shapes = (
        jax.ShapeDtypeStruct(f.shape, f32),
        jax.ShapeDtypeStruct(f.shape, f32),
        jax.ShapeDtypeStruct((1,) + block, f32),
    )
    return pl.pallas_call(
        functools.partial(kernel, nr, nc, parts),
        out_shape=tuple(pltpu.VMEM(x.shape, x.dtype) for x in shapes),
        in_specs=[anyspace] * 5 + [smem] + [anyspace] * 3 + [smem] + [anyspace] * 2,
        out_specs=(anyspace,) * 3,
        scratch_shapes=[
            pltpu.VMEM(block, f32),
            pltpu.VMEM((pb, blk, blk), f32),
            pltpu.VMEM((slots, blk, blk), f32),
            pltpu.VMEM((bslots, blk, blk), f32),
            pltpu.VMEM((pb, 2 * blk, 2 * blk), bf16),
            pltpu.VMEM((slots, 2 * blk, 2 * blk), bf16),
            pltpu.VMEM((bslots, 2 * blk, 2 * blk), bf16),
            pltpu.VMEM((3, parts, nr) + some, f32),
            pltpu.VMEM((nr * pb, some[1], 2 * blk), bf16),
            pltpu.VMEM((slots, some[1], blk), f32),
            pltpu.VMEM((2, parts, nc) + some, f32),
            pltpu.VMEM((2, parts, nc) + some, f32),
            pltpu.VMEM((parts, nc) + some, f32),
            pltpu.VMEM((pb * blk, pb * blk), bf16),
            pltpu.VMEM(block, f32),
            pltpu.VMEM(block, f32),
            pltpu.VMEM(block, f32),
            pltpu.SMEM((slots,), jnp.int32),
            pltpu.SMEM((bslots,), jnp.int32),
            pltpu.SMEM(src.shape, jnp.int32),
            pltpu.SMEM(tgt.shape, jnp.int32),
            pltpu.SMEM(clu.shape, jnp.int32),
            pltpu.SMEM(btgt.shape, jnp.int32),
            pltpu.VMEM(w.shape, f32),
            pltpu.VMEM(lab.shape, jnp.int32),
            dma((3,)),
            dma((6,)),
            dma((chunks,)),
            dma((3,)),
            dma((3, parts, nr)),
            dma((3, parts, nr)),
            dma((3, parts, nc)),
            dma((3, parts, nc)),
        ],
        compiler_params=pltpu.CompilerParams(
            collective_id=0, has_side_effects=True, vmem_limit_bytes=vmem_bytes
        ),
        cost_estimate=pl.CostEstimate(
            flops=flops, bytes_accessed=4 * blk * blk * (slots + bslots + pb), transcendentals=0
        ),
    )(f, d, a, src, tgt, cnt, b, clu, btgt, bcnt, w, lab)


def solution(mesh):
    tensor = P("row", "col", None, None, None)
    index = P("row", "col", None)
    plain = P("row", "col", None, None)
    tally = P("row", "col")
    return jax.shard_map(
        functools.partial(body, mesh.shape["row"], mesh.shape["col"]),
        mesh=mesh,
        in_specs=(tensor, tensor, tensor, index, index, tally, tensor, index, index, tally, plain, plain),
        out_specs=(tensor, tensor, P("row", None, None, None)),
        check_vma=False,
    )
```

time: 50.3 us -> 37.7 us (0.75)
  local copies, waits for them, and re-layouts: 10.3 us -> 1.85 us
  Pallas kernels: 37.7 us -> 33.7 us
    unnamed x23 -> x3, local copies, waits for them, and re-layouts: 10.3 us -> 1.85 us
    pallas_call x1, Pallas kernels: 37.7 us -> 33.7 us  [body(): pl.pallas_call(functools.partial(kernel, nr, nc, parts), out_shape=tuple(...]
where the time goes in v2:
time: 37.7 us; the launch traced here: 37.5 us
  Pallas kernels  33.7 us (89%)
  between operations  1.93 us (5%)
  local copies, waits for them, and re-layouts  1.85 us (5%)
    pallas_call x1, Pallas kernels, body(): pl.pallas_call(functools.partial(kernel, nr, nc, parts), out_shape=tuple(...  33.7 us
    unnamed x3, local copies, waits for them, and re-layouts  1.85 us

profile of v2, /device:TPU:0, one launch (start us, length us, event | category | flops | bytes accessed | tf_op | source)
XLA Modules:
  0.0 37.5 jit_solution(3967695487665101347)
XLA Ops:
  1.9 33.7 %shard_map.139 = (f32[1,1,2,32,128]{4,3,2,1,0:T(8,128)S(1)}, f32[1,1,2,32,128]{4,3,2,1,0:T(8,128)S(1)}, f32[1,2,32,128]{3,2,1,0:T(8,128)S(1)}) custom-call(f32[1,1,2,32,128]{4,3,2,1,0:T(8,128)} %f_hbm.1, f32[1,1,2,128,128]{4,3,2,1,0:T(8,128)} %d_hbm.1, f32[1,1,32,128,128]{4,3,2,1,0:T(8,128)} %a_hbm.1, s32[1,1,32]{2,1,0:T(1,128)} %src_h.1, ...), custom_call_target="tpu_custom_call" | custom-call | flops 360710144 | bytes 3276800 | tf_op jit(solution)/shard_map/pallas_call | solution.py:329
  35.7 0.6 %copy.18 = f32[1,1,2,32,128]{4,3,2,1,0:T(8,128)} copy(f32[1,1,2,32,128]{4,3,2,1,0:T(8,128)S(1)} %get-tuple-element.3) | data formatting | bytes 65536
  36.3 0.6 %copy.19 = f32[1,1,2,32,128]{4,3,2,1,0:T(8,128)} copy(f32[1,1,2,32,128]{4,3,2,1,0:T(8,128)S(1)} %get-tuple-element.4) | data formatting | bytes 65536
  36.9 0.6 %copy.20 = f32[1,2,32,128]{3,2,1,0:T(8,128)} copy(f32[1,2,32,128]{3,2,1,0:T(8,128)S(1)} %get-tuple-element.5) | data formatting | bytes 65536

commit v3 on v2

--- a/solution.py
+++ b/solution.py
@@ -11,7 +11,7 @@
 MESH = pl.DeviceIdType.MESH
 f32, bf16 = jnp.float32, jnp.bfloat16
 unrolled_most = 8
-slot_group = 8
+slot_group = 16
 vmem_bytes = 60 * 1024 * 1024
 halves = 2
 
@@ -213,11 +213,11 @@
         a_in[c].wait()
 
         def prepare_a(j, carry):
-            prepare(wa, c * per + 2 * j, a_v[c * per + 2 * j])
-            prepare(wa, c * per + 2 * j + 1, a_v[c * per + 2 * j + 1])
-            return carry
-
-        lax.fori_loop(0, per // 2, prepare_a, 0)
+            for i in range(4):
+                prepare(wa, c * per + 4 * j + i, a_v[c * per + 4 * j + i])
+            return carry
+
+        lax.fori_loop(0, per // 4, prepare_a, 0)
 
     for copy in small:
         copy.wait()
@@ -233,7 +233,8 @@
     b_in.wait()
 
     def prepare_b(j, carry):
-        prepare(wb, j, b_v[j])
+        for i in range(4):
+            prepare(wb, 4 * j + i, b_v[4 * j + i])
         return carry
 
     def keep_b(s, carry):
@@ -251,7 +252,7 @@
     x_copy = pltpu.make_async_copy(x_v, x_out.at[0, 0], out_sem.at[0])
     x_copy.start()
 
-    lax.fori_loop(0, bslots, prepare_b, 0)
+    lax.fori_loop(0, bslots // 4, prepare_b, 0)
     lax.fori_loop(0, bslots, keep_b, 0)
     aggregate = lax.broadcasted_iota(jnp.int32, (pb * blk, blk), 0)
     for p in range(pb):

time: 37.7 us -> 37.4 us (level)
  no operation moved by 1% of the time
where the time goes in v3:
time: 37.4 us; the launch traced here: 37.3 us
  Pallas kernels  33.5 us (90%)
  between operations  1.93 us (5%)
  local copies, waits for them, and re-layouts  1.85 us (5%)
    pallas_call x1, Pallas kernels, body(): pl.pallas_call(functools.partial(kernel, nr, nc, parts), out_shape=tuple(...  33.5 us
    unnamed x3, local copies, waits for them, and re-layouts  1.85 us

profile of v3, /device:TPU:0, one launch (start us, length us, event | category | flops | bytes accessed | tf_op | source)
XLA Modules:
  0.0 37.3 jit_solution(18289565325306574519)
XLA Ops:
  1.9 33.5 %shard_map.139 = (f32[1,1,2,32,128]{4,3,2,1,0:T(8,128)S(1)}, f32[1,1,2,32,128]{4,3,2,1,0:T(8,128)S(1)}, f32[1,2,32,128]{3,2,1,0:T(8,128)S(1)}) custom-call(f32[1,1,2,32,128]{4,3,2,1,0:T(8,128)} %f_hbm.1, f32[1,1,2,128,128]{4,3,2,1,0:T(8,128)} %d_hbm.1, f32[1,1,32,128,128]{4,3,2,1,0:T(8,128)} %a_hbm.1, s32[1,1,32]{2,1,0:T(1,128)} %src_h.1, ...), custom_call_target="tpu_custom_call" | custom-call | flops 360710144 | bytes 3276800 | tf_op jit(solution)/shard_map/pallas_call | solution.py:330
  35.4 0.6 %copy.18 = f32[1,1,2,32,128]{4,3,2,1,0:T(8,128)} copy(f32[1,1,2,32,128]{4,3,2,1,0:T(8,128)S(1)} %get-tuple-element.3) | data formatting | bytes 65536
  36.0 0.6 %copy.19 = f32[1,1,2,32,128]{4,3,2,1,0:T(8,128)} copy(f32[1,1,2,32,128]{4,3,2,1,0:T(8,128)S(1)} %get-tuple-element.4) | data formatting | bytes 65536
  36.6 0.6 %copy.20 = f32[1,2,32,128]{3,2,1,0:T(8,128)} copy(f32[1,2,32,128]{3,2,1,0:T(8,128)S(1)} %get-tuple-element.5) | data formatting | bytes 65536
